TPU v7x, 32 devices: a whole 2x2x4 slice. The times are simulated.
32 devices in a mesh: inline: 2 (over y), window: 4 (over z), replica: 4 (over x, core).
Axes of the slice: x: 2, y: 2, z: 4, core: 2. Of those that a mesh axis runs over, the one named last changes fastest.
Arguments:
- tokens: bfloat16 [64, 128, 8, 512], P(('replica', 'inline', 'window')), parts along dimension 0, may hold values from -6 to 6
- probe_match_payload_matrix: bfloat16 [512, 1536], replicated, may hold values from -1.5 to 1.5
- w_out: bfloat16 [512, 512], replicated, may hold values from -0.25 to 0.25
Outputs:
- update: bfloat16 [64, 128, 8, 512], P(('replica', 'inline', 'window')), parts along dimension 0
There are 4 independent parts, one for each index of `replica`. A program takes and returns all parts, laid end to end along the dimension named above; an argument that names none is the same for every part. Nothing has to cross between parts.
All inputs are finite; a program needn't handle non-finite values.
Results may differ from a plain program's by a relative error of at most 0.012.
The roundings to bfloat16 on the way count: a program that leaves them out, or rounds other values in their place, can miss the bound.
Values may be sent and summed in bfloat16 or wider, within the bound.
A program may use at most 64 MiB of HBM per device.

v0:
```python
import jax
import jax.numpy as jnp
from jax import lax
from jax.sharding import PartitionSpec as P

EMBED_SPAN = 512
FOCUS_GROUPS = 16
WIN = 8


EPSILON = 1e-05


def standardize_features(payload_vectors):
    center = payload_vectors - jnp.mean(payload_vectors, axis=-1, keepdims=True)
    spread = jnp.mean(center * center, axis=-1, keepdims=True)
    return center * lax.rsqrt(spread + EPSILON)


def to_windows(block):
    first, second, third, width = block.shape
    shaped = block.reshape(first // WIN, WIN, second // WIN, WIN, third // WIN, WIN, width)
    return shaped.transpose(0, 2, 4, 1, 3, 5, 6).reshape(-1, WIN * WIN * WIN, width)


def from_windows(cube_rows, first, second, third):
    width = cube_rows.shape[-1]
    shaped = cube_rows.reshape(first // WIN, second // WIN, third // WIN, WIN, WIN, WIN, width)
    return shaped.transpose(0, 3, 1, 4, 2, 5, 6).reshape(first, second, third, width)


def ingest_summary(running_state, condensed_question_series, lookup_arrays, payload_vectors):
    top_old, total_old, summed_old = running_state
    reduced_dimension = EMBED_SPAN // FOCUS_GROUPS
    softmax_sharpness = reduced_dimension ** (-0.5)
    probe_split = condensed_question_series.reshape(
        condensed_question_series.shape[0], FOCUS_GROUPS, reduced_dimension
    )
    lookup_divided = lookup_arrays.reshape(lookup_arrays.shape[0], FOCUS_GROUPS, reduced_dimension)
    payload_split = payload_vectors.reshape(
        payload_vectors.shape[0], FOCUS_GROUPS, reduced_dimension
    )
    similarity_raw_scores = (
        jnp.einsum("xjr,ijr->jxi", probe_split, lookup_divided, preferred_element_type=jnp.float32)
        * softmax_sharpness
    )
    top_new = jnp.maximum(top_old, jnp.max(similarity_raw_scores, axis=-1))
    rescale = jnp.exp(top_old - top_new)
    weights = jnp.exp(similarity_raw_scores - top_new[..., None])
    total_new = jnp.sum(weights, axis=-1)
    added = jnp.einsum(
        "hqk,khd->qhd",
        weights.astype(jnp.bfloat16),
        payload_split,
        preferred_element_type=jnp.float32,
    )
    summed_new = summed_old * rescale.T[:, :, None] + added
    return (top_new, total_new, summed_new)


def tile_mixing(
    tile_items,
    probe_match_payload_matrix,
    digest_match_list,
    digest_payload_list,
    broad_contribution,
):
    count = tile_items.shape[0]
    reduced_dimension = EMBED_SPAN // FOCUS_GROUPS
    softmax_sharpness = reduced_dimension ** (-0.5)
    projected = jnp.dot(
        tile_items, probe_match_payload_matrix, preferred_element_type=jnp.float32
    ).astype(jnp.bfloat16)
    question_arrays = projected[:, :EMBED_SPAN].reshape(count, FOCUS_GROUPS, reduced_dimension)
    lookup_arrays = projected[:, EMBED_SPAN : 2 * EMBED_SPAN].reshape(
        count, FOCUS_GROUPS, reduced_dimension
    )
    payload_vectors = projected[:, 2 * EMBED_SPAN :].reshape(count, FOCUS_GROUPS, reduced_dimension)
    lookup_condensed = digest_match_list.reshape(FOCUS_GROUPS, reduced_dimension)
    payload_digest = digest_payload_list.reshape(FOCUS_GROUPS, reduced_dimension).astype(
        jnp.float32
    )
    per_group = FOCUS_GROUPS // 4
    results = []
    for head_group in range(4):
        bottom_bound = head_group * per_group
        ceiling_bound = bottom_bound + per_group
        similarity_raw_scores = (
            jnp.einsum(
                "xjr,ijr->jxi",
                question_arrays[:, bottom_bound:ceiling_bound],
                lookup_arrays[:, bottom_bound:ceiling_bound],
                preferred_element_type=jnp.float32,
            )
            * softmax_sharpness
        )
        courier_marks = (
            jnp.einsum(
                "yoc,oc->oy",
                question_arrays[:, bottom_bound:ceiling_bound],
                lookup_condensed[bottom_bound:ceiling_bound],
                preferred_element_type=jnp.float32,
            )
            * softmax_sharpness
        )
        top = jnp.maximum(jnp.max(similarity_raw_scores, axis=-1), courier_marks)
        weights = jnp.exp(similarity_raw_scores - top[..., None])
        car_weights = jnp.exp(courier_marks - top)
        total = jnp.sum(weights, axis=-1) + car_weights
        summed = jnp.einsum(
            "hqk,khd->qhd",
            weights.astype(jnp.bfloat16),
            payload_vectors[:, bottom_bound:ceiling_bound],
            preferred_element_type=jnp.float32,
        )
        car_rounded = car_weights.astype(jnp.bfloat16).astype(jnp.float32)
        summed = (
            summed
            + car_rounded.T[:, :, None] * payload_digest[bottom_bound:ceiling_bound][None, :, :]
        )
        results.append(summed / total.T[:, :, None])
    local = jnp.concatenate(results, axis=1).reshape(count, EMBED_SPAN)
    return (local + broad_contribution[None, :]).astype(jnp.bfloat16)


def body(tokens, probe_match_payload_matrix, w_out):
    reduced_dimension = EMBED_SPAN // FOCUS_GROUPS
    entry_rows, entry_cols, entry_depth, width = tokens.shape
    normed = standardize_features(tokens.astype(jnp.float32)).astype(jnp.bfloat16)
    grouped = lax.all_to_all(normed, "window", split_axis=1, concat_axis=0, tiled=True)
    block_rows, block_cols, block_depth, width = grouped.shape
    tile_entries = to_windows(grouped)
    own_count = tile_entries.shape[0]
    averaged_tiles = jnp.sum(tile_entries.astype(jnp.float32), axis=1) / (
        1.0 * tile_entries.shape[1]
    )
    digest_items = standardize_features(averaged_tiles).astype(jnp.bfloat16)
    digest_mapping = jnp.dot(
        digest_items, probe_match_payload_matrix, preferred_element_type=jnp.float32
    ).astype(jnp.bfloat16)
    condensed_question_series = digest_mapping[:, :EMBED_SPAN]
    digest_match_list = digest_mapping[:, EMBED_SPAN : 2 * EMBED_SPAN]
    digest_payload_list = digest_mapping[:, 2 * EMBED_SPAN :]
    initial_state = (
        jnp.full((FOCUS_GROUPS, own_count), -1e30, jnp.float32),
        jnp.zeros((FOCUS_GROUPS, own_count), jnp.float32),
        jnp.zeros((own_count, FOCUS_GROUPS, reduced_dimension), jnp.float32),
    )
    match_payload_pair = jnp.dot(
        lax.all_gather(digest_items, ("inline", "window"), axis=0, tiled=True),
        probe_match_payload_matrix[:, EMBED_SPAN:],
        preferred_element_type=jnp.float32,
    ).astype(jnp.bfloat16)
    folded = ingest_summary(
        initial_state,
        condensed_question_series,
        match_payload_pair[:, :EMBED_SPAN],
        match_payload_pair[:, EMBED_SPAN:],
    )
    broad_context = (folded[2] / folded[1].T[:, :, None]).reshape(own_count, EMBED_SPAN)

    def single_tile(window_item):
        return tile_mixing(
            window_item[0],
            probe_match_payload_matrix,
            window_item[1],
            window_item[2],
            window_item[3],
        )

    nested_step = lax.map(
        single_tile, (tile_entries, digest_match_list, digest_payload_list, broad_context)
    )
    projected = jnp.dot(
        nested_step.reshape(-1, width), w_out, preferred_element_type=jnp.float32
    ).astype(jnp.bfloat16)
    placed = from_windows(projected.reshape(nested_step.shape), block_rows, block_cols, block_depth)
    returned = lax.all_to_all(placed, "window", split_axis=0, concat_axis=1, tiled=True)
    return returned


def solution(mesh):
    return jax.shard_map(
        body,
        mesh=mesh,
        in_specs=(P(("replica", "inline", "window"), None, None, None), P(), P()),
        out_specs=P(("replica", "inline", "window"), None, None, None),
        check_vma=False,
    )
```

profile of v0, /device:TPU:0, one launch (start us, length us, event | category | flops | bytes accessed | tf_op | source)
XLA Modules:
  0.0 308.6 jit_solution(11959476698765880580)
XLA Ops:
  6.7 6.3 %all-to-all-start = ((bf16[2,128,8,512]{3,2,0,1:T(8,128)(2,1)}), bf16[2,128,8,512]{3,2,0,1:T(8,128)(2,1)S(1)}, u32[]{:S(2)}, u32[]{:S(2)}) async-start(bf16[2,128,8,512]{3,2,0,1:T(8,128)(2,1)} %fusion.88), calls=%async_computation | async-start | bytes 4194304 | tf_op jit(solution)/shard_map/all_to_all | solution.py:130
  13.0 48.2 %all-to-all-done = bf16[2,128,8,512]{3,2,0,1:T(8,128)(2,1)S(1)} async-done(((bf16[2,128,8,512]{3,2,0,1:T(8,128)(2,1)}), bf16[2,128,8,512]{3,2,0,1:T(8,128)(2,1)S(1)}, u32[]{:S(2)}, u32[]{:S(2)}) %all-to-all-start) | async-done | bytes 2097184 | tf_op jit(solution)/shard_map/all_to_all | solution.py:130
  65.5 30.4 %all-gather = bf16[8,4,512]{2,1,0:T(4,128)(2,1)S(1)} all-gather(bf16[1,4,512]{2,1,0:T(4,128)(2,1)S(1)} %fusion.129), channel_id=1, replica_groups=mesh['inline'=2,'window'=4,'replica'=4] {'inline','window'}, dimensions={0}, use_global_device_ids=true | all-gather | bytes 36864 | tf_op jit(solution)/shard_map/all_gather | solution.py:150
  98.6 161.6 %while.10 = (s32[]{:T(128)}, bf16[4,512,512]{2,1,0:T(8,128)(2,1)}, bf16[4,512,512]{2,1,0:T(8,128)(2,1)}, bf16[512,1536]{1,0:T(8,128)(2,1)}, bf16[4,512]{1,0:T(4,...) while((s32[]{:T(128)}, bf16[4,512,512]{2,1,0:T(8,128)(2,1)}, ...), condition=%wide.region_16.17_spmd, body=%wide.region_7.16_spmd.sunk | while | flops 1379189248 | bytes 74441896 | solution.py:171
  101.8 2.7 multiply_reduce_fusion.13
  104.8 2.9 fusion.209
  108.1 3.0 fusion.210
  111.1 2.7 multiply_reduce_fusion.12
  114.0 2.9 fusion.205
  117.0 3.0 fusion.206
  120.0 2.7 multiply_reduce_fusion.11
  122.9 2.9 fusion.201
  125.9 3.0 fusion.202
  128.9 2.7 multiply_reduce_fusion.10
  131.8 2.9 fusion.197
  134.8 3.0 fusion.198
  142.2 2.7 multiply_reduce_fusion.13
  145.2 2.9 fusion.209
  148.5 3.0 fusion.210
  151.4 2.7 multiply_reduce_fusion.12
  154.4 2.9 fusion.205
  157.3 3.0 fusion.206
  163.2 2.9 fusion.201
  166.2 3.0 fusion.202
  172.1 2.9 fusion.197
  175.1 3.0 fusion.198
  182.5 2.7 multiply_reduce_fusion.13
  185.6 2.9 fusion.209
  188.8 3.0 fusion.210
  191.8 2.7 multiply_reduce_fusion.12
  194.7 2.9 fusion.205
  197.7 3.0 fusion.206
  203.6 2.9 fusion.201
  206.6 3.0 fusion.202
  212.5 2.9 fusion.197
  215.5 3.0 fusion.198
  222.9 2.7 multiply_reduce_fusion.13
  225.9 2.9 fusion.209
  229.2 3.0 fusion.210
  235.1 2.9 fusion.205
  238.1 3.0 fusion.206
  243.9 2.9 fusion.201
  246.9 3.0 fusion.202
  249.9 2.7 multiply_reduce_fusion.10
  252.8 2.9 fusion.197
  255.8 3.0 fusion.198
  260.1 2.8 convolution_convert_fusion.1
  263.2 43.9 %all_to_all.33 = bf16[8,32,8,512]{3,2,1,0:T(8,128)(2,1)S(1)} all-to-all(bf16[8,32,8,512]{3,2,1,0:T(8,128)(2,1)S(1)} %bitcast.285), channel_id=1, replica_groups=mesh['inline'=2,'window'=4,'replica'=4] {'window'}, dimensions={0} | all-to-all | bytes 4194304 | tf_op jit(solution)/shard_map/all_to_all | solution.py:178
  (172 shorter events, 55.4 us)
Async XLA Ops:
  0.0 260.1 %copy-start = (bf16[512,512]{1,0:T(8,128)(2,1)S(1)}, bf16[512,512]{1,0:T(8,128)(2,1)}, u32[]{:S(2)}) copy-start(bf16[512,512]{1,0:T(8,128)(2,1)} %param.7) | copy-start | bytes 1572868
  0.0 4.9 %copy-start.1 = (bf16[2,128,8,512]{3,2,1,0:T(8,128)(2,1)S(1)}, bf16[2,128,8,512]{3,2,1,0:T(8,128)(2,1)}, u32[]{:S(2)}) copy-start(bf16[2,128,8,512]{3,2,1,0:T(8,128)(2,1)} %param.5) | copy-start | bytes 6291460
  6.7 54.5 %all-to-all-start = ((bf16[2,128,8,512]{3,2,0,1:T(8,128)(2,1)}), bf16[2,128,8,512]{3,2,0,1:T(8,128)(2,1)S(1)}, u32[]{:S(2)}, u32[]{:S(2)}) async-start(bf16[2,128,8,512]{3,2,0,1:T(8,128)(2,1)} %fusion.88), calls=%async_computation | async-start | bytes 4194304 | tf_op jit(solution)/shard_map/all_to_all | solution.py:130
where the time goes:
time: 310 us; the launch traced here: 309 us
  matrix products  109 us (35%)
  blocking collectives  74.3 us (24%)
  other arithmetic  55.1 us (18%)
  waiting for transfers between devices  48.2 us (16%)
  local copies, waits for them, and re-layouts  14.4 us (5%)
  starting transfers between devices  6.32 us (2%)
    all_to_all x1, waiting for transfers between devices, body(): lax.all_to_all(normed, 'window', split_axis=1, concat_axis=0, tiled=True)  48.2 us
    dot_general x16, matrix products, tile_mixing(): jnp.einsum('hqk,khd->qhd', weights.astype(jnp.bfloat16), payload_vectors[...  47.6 us
    reduce_sum x16, other arithmetic, tile_mixing(): total = jnp.sum(weights, axis=-1) + car_weights  46.3 us
    all_to_all x1, blocking collectives, body(): lax.all_to_all(placed, 'window', split_axis=0, concat_axis=1, tiled=True)  43.9 us
    dot_general x16, matrix products, tile_mixing(): jnp.einsum('xjr,ijr->jxi', question_arrays[:, bottom_bound:ceiling_bound]...  42.9 us
    all_gather x1, blocking collectives, body(): lax.all_gather(digest_items, ('inline', 'window'), axis=0, tiled=True)  30.4 us
    dot_general x4, matrix products, tile_mixing(): jnp.dot(tile_items, probe_match_payload_matrix, preferred_element_type=jn...  10.2 us
    all_to_all x1, starting transfers between devices, body(): lax.all_to_all(normed, 'window', split_axis=1, concat_axis=0, tiled=True)  6.32 us
  transfers between devices with their start and end apart: 1, of which 1 were waited for; matrix products, arithmetic and copies ran while one was open for 0% of the time, Pallas kernels for 0%

commit v1 on v0

v1 whole, which is shorter than its diff:
```python
import functools

import jax
import jax.numpy as jnp
from jax import lax
from jax.experimental import pallas as pl
from jax.experimental.pallas import tpu as pltpu
from jax.sharding import PartitionSpec as P

EMBED_SPAN = 512
FOCUS_GROUPS = 16
HEAD = EMBED_SPAN // FOCUS_GROUPS
WIN = 8
EPSILON = 1e-05
MESH = pl.DeviceIdType.MESH
F32 = jnp.float32
BF16 = jnp.bfloat16


def standardize(x):
    center = x - jnp.mean(x, axis=-1, keepdims=True)
    spread = jnp.mean(center * center, axis=-1, keepdims=True)
    return center * lax.rsqrt(spread + EPSILON)


def window_peers(me, n):
    if n % 2:
        return [lax.rem(me + o, n) for o in range(1, n)]
    same = [lax.rem(me + o, n) for o in range(2, n, 2)]
    odd = [lax.rem(n + c - me, n) for c in range(n - 1, 0, -2)]
    return same + odd


def kernel(
    n_in, n_win, rows, strips,
    tok_ref, w_ref, wo_ref, out_ref,
    normed, xin, ybuf, psum, cars, wq_t, wv_t, k_buf, q_t, v_t, in_t, glob_buf, kcar_buf, vcar_buf,
    fsend, frecv, bsend, brecv, psend, precv, csend, crecv, lsem, blsem,
):
    ii = lax.axis_index("inline")
    me = lax.axis_index("window")
    span = strips // n_win
    npos = WIN // rows
    n_ci = n_win // npos
    own = span * n_ci
    group_cars = n_ci * strips
    width = EMBED_SPAN
    tokens = WIN * WIN * WIN
    my_ci = me // npos
    my_pos = lax.rem(me, npos)
    peers = window_peers(me, n_win)
    in_peers = [lax.rem(ii + o, n_in) for o in range(1, n_in)]

    barrier = pltpu.get_barrier_semaphore()
    for d in peers:
        pl.semaphore_signal(barrier, inc=1, device_id={"window": d}, device_id_type=MESH)
    for d in in_peers:
        pl.semaphore_signal(barrier, inc=1, device_id={"inline": d}, device_id_type=MESH)

    def norm_strip(cx, carry):
        x = standardize(tok_ref[:, cx].astype(F32)).astype(BF16)
        normed[cx] = x
        part = jnp.sum(x.astype(F32), axis=(0, 1))
        psum[me, pl.ds(cx, 1), :] = part[None, :]
        return carry

    lax.fori_loop(0, strips, norm_strip, 0)
    pl.semaphore_wait(barrier, len(peers) + len(in_peers))

    def p_copy(k, d, src):
        return pltpu.make_async_remote_copy(
            src_ref=psum.at[src], dst_ref=psum.at[src], send_sem=psend.at[k], recv_sem=precv.at[src],
            device_id={"window": d}, device_id_type=MESH,
        )

    def f_copy(k, j, d, src):
        return pltpu.make_async_remote_copy(
            src_ref=normed.at[d * span + j], dst_ref=xin.at[(src // npos) * span + j, lax.rem(src, npos)],
            send_sem=fsend.at[k, j], recv_sem=frecv.at[src, j],
            device_id={"window": d}, device_id_type=MESH,
        )

    def l_copy(j):
        return pltpu.make_async_copy(
            normed.at[me * span + j], xin.at[my_ci * span + j, my_pos], lsem.at[j]
        )

    for k, d in enumerate(peers):
        p_copy(k, d, me).start()
    for j in range(span):
        for k, d in enumerate(peers):
            f_copy(k, j, d, me).start()
        l_copy(j).start()

    wq_t[...] = w_ref[:, :width].T
    wv_t[...] = w_ref[:, 2 * width :].T

    for d in peers:
        p_copy(0, d, d).wait_recv()
    for ci in range(n_ci):
        total = psum[ci * npos]
        for p in range(1, npos):
            total = total + psum[ci * npos + p]
        cars[ii, pl.ds(ci * strips, strips), :] = standardize(total * (1.0 / tokens)).astype(BF16)

    def c_copy(k, d, src):
        return pltpu.make_async_remote_copy(
            src_ref=cars.at[src], dst_ref=cars.at[src], send_sem=csend.at[k], recv_sem=crecv.at[src],
            device_id={"inline": d}, device_id_type=MESH,
        )

    for k, d in enumerate(in_peers):
        c_copy(k, d, ii).start()

    scale = HEAD ** (-0.5)
    mine = jnp.dot(cars[ii], w_ref[...], preferred_element_type=F32).astype(BF16)
    kcar_buf[...] = mine[:, width : 2 * width].astype(F32)
    vcar_buf[...] = mine[:, 2 * width :].astype(F32)
    for d in in_peers:
        c_copy(0, d, d).wait_recv()
    every = cars[...].reshape(n_in * group_cars, width)
    kv = jnp.dot(every, w_ref[:, width:], preferred_element_type=F32).astype(BF16)
    col_head = lax.broadcasted_iota(jnp.int32, (group_cars, width), 1) // HEAD
    q_car = mine[:, :width].astype(F32)
    glob = jnp.zeros((group_cars, width), F32)
    for h in range(FOCUS_GROUPS):
        q_h = jnp.where(col_head == h, q_car, 0.0).astype(BF16)
        s = lax.dot_general(q_h, kv[:, :width], (((1,), (1,)), ((), ())), preferred_element_type=F32) * scale
        e = jnp.exp(s - jnp.max(s, axis=-1, keepdims=True))
        t = jnp.sum(e, axis=-1, keepdims=True)
        o = jnp.dot(e.astype(BF16), kv[:, width:], preferred_element_type=F32) / t
        glob = jnp.where(col_head == h, o, glob)
    glob_buf[...] = glob

    def b_copy(slot, p, dst, owner, j):
        return pltpu.make_async_remote_copy(
            src_ref=ybuf.at[slot, p], dst_ref=out_ref.at[:, owner * span + j],
            send_sem=bsend.at[slot, p], recv_sem=brecv.at[owner, j],
            device_id={"window": dst}, device_id_type=MESH,
        )

    def bl_copy(slot, j):
        return pltpu.make_async_copy(ybuf.at[slot, my_pos], out_ref.at[:, me * span + j], blsem.at[j])

    def cube(slot, carry):
        ci = slot // span
        j = lax.rem(slot, span)
        for p in range(npos):
            src = ci * npos + p

            @pl.when(src != me)
            def _():
                f_copy(0, j, me, src).wait_recv()

            @pl.when(src == me)
            def _():
                l_copy(j).wait()

        x = xin[slot].reshape(tokens, width)
        row = ci * strips + me * span + j
        pick = lax.broadcasted_iota(jnp.int32, (group_cars, width), 0) == row

        def chosen(ref):
            return jnp.sum(jnp.where(pick, ref[...], 0.0), axis=0, keepdims=True)

        def column(r):
            return jnp.broadcast_to(r, (128, width)).T[:, :1]

        k_buf[:tokens, :] = jnp.dot(x, w_ref[:, width : 2 * width], preferred_element_type=F32).astype(BF16)
        k_buf[tokens:, :] = jnp.broadcast_to(chosen(kcar_buf), (16, width)).astype(BF16)
        nt = (((1,), (1,)), ((), ()))
        q_t[...] = lax.dot_general(wq_t[...], x, nt, preferred_element_type=F32).astype(BF16)
        v_t[...] = lax.dot_general(wv_t[...], x, nt, preferred_element_type=F32).astype(BF16)
        glob_col = column(chosen(glob_buf))
        vcar_col = column(chosen(vcar_buf))
        for hb in range(width // 128):
            kb = k_buf[:, hb * 128 : (hb + 1) * 128]
            for h4 in range(128 // HEAD):
                lo = hb * 128 + h4 * HEAD
                parts = [q_t[lo : lo + HEAD, :]]
                if h4:
                    parts.insert(0, jnp.zeros((h4 * HEAD, tokens), BF16))
                if h4 < 128 // HEAD - 1:
                    parts.append(jnp.zeros((128 - (h4 + 1) * HEAD, tokens), BF16))
                s = jnp.dot(kb, jnp.concatenate(parts, axis=0), preferred_element_type=F32)
                s_car = s[tokens : tokens + 1]
                s = s[:tokens]
                top = jnp.maximum(jnp.max(s, axis=0, keepdims=True), s_car)
                e = jnp.exp((s - top) * scale)
                e_car = jnp.exp((s_car - top) * scale)
                total = jnp.sum(e, axis=0, keepdims=True) + e_car
                o = jnp.dot(v_t[lo : lo + HEAD, :], e.astype(BF16), preferred_element_type=F32)
                o = o + vcar_col[lo : lo + HEAD] * e_car.astype(BF16).astype(F32)
                in_t[lo : lo + HEAD, :] = (o / total + glob_col[lo : lo + HEAD]).astype(BF16)
        inner = in_t[...].T
        upd = jnp.dot(inner, wo_ref[...], preferred_element_type=F32).astype(BF16)
        ybuf[slot] = upd.reshape(npos, rows, WIN * WIN, width)
        for p in range(npos):
            dst = ci * npos + p

            @pl.when(dst != me)
            def _():
                b_copy(slot, p, dst, me, j).start()

            @pl.when(dst == me)
            def _():
                bl_copy(slot, j).start()

        return carry

    lax.fori_loop(0, own, cube, 0)

    for k, d in enumerate(peers):
        p_copy(k, d, me).wait_send()
    for k, d in enumerate(in_peers):
        c_copy(k, d, ii).wait_send()
    for j in range(span):
        for k, d in enumerate(peers):
            f_copy(k, j, d, me).wait_send()
    for j in range(span):
        for d in peers:
            b_copy(0, 0, me, d, j).wait_recv()
        bl_copy(my_ci * span + j, j).wait()
    for slot in range(own):
        for p in range(npos):
            dst = (slot // span) * npos + p

            @pl.when(dst != me)
            def _():
                b_copy(slot, p, dst, me, slot % span).wait_send()


def body(n_in, n_win, tokens, w, w_out):
    rows, xl, dep, width = tokens.shape
    strips = xl // WIN
    npos = WIN // rows
    span = strips // n_win
    own = span * (n_win // npos)
    group_cars = (n_win // npos) * strips
    cube = WIN * WIN * WIN
    block = (rows, WIN * WIN, width)
    vmem = pl.BlockSpec(memory_space=pltpu.VMEM)
    dma = pltpu.SemaphoreType.DMA
    shaped = tokens.reshape(rows, strips, WIN * dep, width)
    out = pl.pallas_call(
        functools.partial(kernel, n_in, n_win, rows, strips),
        out_shape=jax.ShapeDtypeStruct(shaped.shape, BF16),
        in_specs=[vmem, vmem, vmem],
        out_specs=pl.BlockSpec(memory_space=pl.ANY),
        scratch_shapes=[
            pltpu.VMEM((strips,) + block, BF16),
            pltpu.VMEM((own, npos) + block, BF16),
            pltpu.VMEM((own, npos) + block, BF16),
            pltpu.VMEM((n_win, strips, width), F32),
            pltpu.VMEM((n_in, group_cars, width), BF16),
            pltpu.VMEM((width, width), BF16),
            pltpu.VMEM((width, width), BF16),
            pltpu.VMEM((cube + 16, width), BF16),
            pltpu.VMEM((width, cube), BF16),
            pltpu.VMEM((width, cube), BF16),
            pltpu.VMEM((width, cube), BF16),
            pltpu.VMEM((group_cars, width), F32),
            pltpu.VMEM((group_cars, width), F32),
            pltpu.VMEM((group_cars, width), F32),
            dma((n_win, span)),
            dma((n_win, span)),
            dma((own, npos)),
            dma((n_win, span)),
            dma((n_win,)),
            dma((n_win,)),
            dma((n_in,)),
            dma((n_in,)),
            dma((span,)),
            dma((span,)),
        ],
        compiler_params=pltpu.CompilerParams(
            collective_id=0, has_side_effects=True, vmem_limit_bytes=48 * 1024 * 1024
        ),
        cost_estimate=pl.CostEstimate(
            flops=2 * own * cube * width * (4 * width + 2 * cube),
            bytes_accessed=4 * own * cube * width,
            transcendentals=own * FOCUS_GROUPS * cube * cube,
        ),
    )(shaped, w, w_out)
    return out.reshape(tokens.shape)


def solution(mesh):
    return jax.shard_map(
        functools.partial(body, mesh.shape["inline"], mesh.shape["window"]),
        mesh=mesh,
        in_specs=(P(("replica", "inline", "window"), None, None, None), P(), P()),
        out_specs=P(("replica", "inline", "window"), None, None, None),
        check_vma=False,
    )
```

time: 310 us -> 106 us (0.34)
  matrix products: 109 us -> 0 us
  Pallas kernels: 0 us -> 102 us
  blocking collectives: 74.3 us -> 0 us
  other arithmetic: 55.1 us -> 0 us
  waiting for transfers between devices: 48.2 us -> 0 us
  local copies, waits for them, and re-layouts: 14.4 us -> 3.77 us
  starting transfers between devices: 6.32 us -> 0 us
    dot_general x57 -> x0, matrix products: 109 us -> none  [the longest x16 47.6 us: tile_mixing(): jnp.einsum('hqk,khd->qhd', weights.astype(jnp.bfloat16), payload_vectors[...]
    pallas_call x0 -> x1, Pallas kernels: none -> 102 us  [body(): pl.pallas_call(functools.partial(kernel, n_in, n_win, rows, strips), out_...]
    reduce_sum x22 -> x0, other arithmetic: 51.8 us -> none  [the longest x16 46.3 us: tile_mixing(): total = jnp.sum(weights, axis=-1) + car_weights]
    all_to_all x1 -> x0, waiting for transfers between devices: 48.2 us -> none  [body(): lax.all_to_all(normed, 'window', split_axis=1, concat_axis=0, tiled=True)]
    all_to_all x1 -> x0, blocking collectives: 43.9 us -> none  [body(): lax.all_to_all(placed, 'window', split_axis=0, concat_axis=1, tiled=True)]
    all_gather x1 -> x0, blocking collectives: 30.4 us -> none  [body(): lax.all_gather(digest_items, ('inline', 'window'), axis=0, tiled=True)]
    all_to_all x1 -> x0, starting transfers between devices: 6.32 us -> none  [body(): lax.all_to_all(normed, 'window', split_axis=1, concat_axis=0, tiled=True)]
    slice x58 -> x0, local copies, waits for them, and re-layouts: 6.21 us -> none  [the longest x20 1.75 us: tile_mixing(): lookup_condensed[bottom_bound:ceiling_bound]]
  transfers between devices with their start and end apart: 1 -> 0, of which waited for: 1 -> 0; matrix products, arithmetic and copies ran while one was open for 0% -> 0% of each run, Pallas kernels for 0% -> 0%
where the time goes in v1:
time: 106 us; the launch traced here: 105 us
  Pallas kernels  102 us (96%)
  local copies, waits for them, and re-layouts  3.77 us (4%)
    pallas_call x1, Pallas kernels, body(): pl.pallas_call(functools.partial(kernel, n_in, n_win, rows, strips), out_...  102 us
    unnamed x5, local copies, waits for them, and re-layouts  3.77 us

profile of v1, /device:TPU:0, one launch (start us, length us, event | category | flops | bytes accessed | tf_op | source)
XLA Modules:
  0.0 105.4 jit_solution(4623696149970576136)
XLA Ops:
  0.0 0.0 copy-start
  0.0 1.4 %copy-done = bf16[512,1536]{1,0:T(8,128)(2,1)S(1)} copy-done((bf16[512,1536]{1,0:T(8,128)(2,1)S(1)}, bf16[512,1536]{1,0:T(8,128)(2,1)}, u32[]{:S(2)}) %copy-start) | copy-done | bytes 1572888
  1.4 0.0 copy-start.1
  1.4 1.0 copy-done.1
  2.5 101.6 %shard_map.37 = bf16[2,16,64,512]{3,2,1,0:T(8,128)(2,1)S(1)} custom-call(bf16[2,16,64,512]{3,2,1,0:T(8,128)(2,1)} %bitcast.3, bf16[512,1536]{1,0:T(8,128)(2,1)S(1)} %copy-done, bf16[512,512]{1,0:T(8,128)(2,1)S(1)} %copy-done.1), custom_call_target="tpu_custom_call" | custom-call | flops 6442450944 | bytes 4194304 | tf_op jit(solution)/shard_map/pallas_call | solution.py:245
  104.1 1.3 %copy.5 = bf16[2,128,8,512]{3,2,1,0:T(8,128)(2,1)} copy(bf16[2,128,8,512]{3,2,1,0:T(8,128)(2,1)S(1)} %bitcast.2) | data formatting | bytes 4194304
Async XLA Ops:
  0.0 1.4 %copy-start = (bf16[512,1536]{1,0:T(8,128)(2,1)S(1)}, bf16[512,1536]{1,0:T(8,128)(2,1)}, u32[]{:S(2)}) copy-start(bf16[512,1536]{1,0:T(8,128)(2,1)} %w_ref.1) | copy-start | bytes 4718596
  1.4 1.0 copy-start.1

commit v2 on v1

--- a/solution.py
+++ b/solution.py
@@ -33,9 +33,10 @@
 
 def kernel(
     n_in, n_win, rows, strips,
-    tok_ref, w_ref, wo_ref, out_ref,
+    tok_ref, w_hbm, wo_hbm, out_ref,
+    tok_buf, w_ref, wo_ref,
     normed, xin, ybuf, psum, cars, wq_t, wv_t, k_buf, q_t, v_t, in_t, glob_buf, kcar_buf, vcar_buf,
-    fsend, frecv, bsend, brecv, psend, precv, csend, crecv, lsem, blsem,
+    fsend, frecv, bsend, brecv, psend, precv, csend, crecv, lsem, blsem, tsem, wsem,
 ):
     ii = lax.axis_index("inline")
     me = lax.axis_index("window")
@@ -57,15 +58,18 @@
     for d in in_peers:
         pl.semaphore_signal(barrier, inc=1, device_id={"inline": d}, device_id_type=MESH)
 
-    def norm_strip(cx, carry):
-        x = standardize(tok_ref[:, cx].astype(F32)).astype(BF16)
-        normed[cx] = x
-        part = jnp.sum(x.astype(F32), axis=(0, 1))
-        psum[me, pl.ds(cx, 1), :] = part[None, :]
-        return carry
-
-    lax.fori_loop(0, strips, norm_strip, 0)
-    pl.semaphore_wait(barrier, len(peers) + len(in_peers))
+    order = [(j, k, d) for j in range(span) for k, d in enumerate(peers + [me])]
+
+    def t_copy(n):
+        j, _, d = order[n]
+        return pltpu.make_async_copy(tok_ref.at[:, d * span + j], tok_buf.at[n], tsem.at[n])
+
+    for n in range(len(order)):
+        t_copy(n).start()
+    w_copy = pltpu.make_async_copy(w_hbm, w_ref, wsem.at[0])
+    wo_copy = pltpu.make_async_copy(wo_hbm, wo_ref, wsem.at[1])
+    w_copy.start()
+    wo_copy.start()
 
     def p_copy(k, d, src):
         return pltpu.make_async_remote_copy(
@@ -85,12 +89,28 @@
             normed.at[me * span + j], xin.at[my_ci * span + j, my_pos], lsem.at[j]
         )
 
+    for n, (j, k, d) in enumerate(order):
+        t_copy(n).wait()
+        x = standardize(tok_buf[n].astype(F32)).astype(BF16)
+        normed[d * span + j] = x
+        psum[me, pl.ds(d * span + j, 1), :] = jnp.sum(x.astype(F32), axis=(0, 1))[None, :]
+        if n == 0:
+            pl.semaphore_wait(barrier, len(peers) + len(in_peers))
+        if j == 0:
+            if k == len(peers):
+                l_copy(j).start()
+            else:
+                f_copy(k, j, d, me).start()
     for k, d in enumerate(peers):
         p_copy(k, d, me).start()
-    for j in range(span):
-        for k, d in enumerate(peers):
-            f_copy(k, j, d, me).start()
-        l_copy(j).start()
+    for j, k, d in order:
+        if j:
+            if k == len(peers):
+                l_copy(j).start()
+            else:
+                f_copy(k, j, d, me).start()
+    w_copy.wait()
+    wo_copy.wait()
 
     wq_t[...] = w_ref[:, :width].T
     wv_t[...] = w_ref[:, 2 * width :].T
@@ -195,7 +215,7 @@
         inner = in_t[...].T
         upd = jnp.dot(inner, wo_ref[...], preferred_element_type=F32).astype(BF16)
         ybuf[slot] = upd.reshape(npos, rows, WIN * WIN, width)
-        for p in range(npos):
+        for p in window_peers(my_pos, npos) + [my_pos]:
             dst = ci * npos + p
 
             @pl.when(dst != me)
@@ -239,15 +259,18 @@
     group_cars = (n_win // npos) * strips
     cube = WIN * WIN * WIN
     block = (rows, WIN * WIN, width)
-    vmem = pl.BlockSpec(memory_space=pltpu.VMEM)
+    hbm = pl.BlockSpec(memory_space=pl.ANY)
     dma = pltpu.SemaphoreType.DMA
     shaped = tokens.reshape(rows, strips, WIN * dep, width)
     out = pl.pallas_call(
         functools.partial(kernel, n_in, n_win, rows, strips),
         out_shape=jax.ShapeDtypeStruct(shaped.shape, BF16),
-        in_specs=[vmem, vmem, vmem],
-        out_specs=pl.BlockSpec(memory_space=pl.ANY),
+        in_specs=[hbm, hbm, hbm],
+        out_specs=hbm,
         scratch_shapes=[
+            pltpu.VMEM((strips,) + block, BF16),
+            pltpu.VMEM(w.shape, BF16),
+            pltpu.VMEM(w_out.shape, BF16),
             pltpu.VMEM((strips,) + block, BF16),
             pltpu.VMEM((own, npos) + block, BF16),
             pltpu.VMEM((own, npos) + block, BF16),
@@ -272,9 +295,11 @@
             dma((n_in,)),
             dma((span,)),
             dma((span,)),
+            dma((strips,)),
+            dma((2,)),
         ],
         compiler_params=pltpu.CompilerParams(
-            collective_id=0, has_side_effects=True, vmem_limit_bytes=48 * 1024 * 1024
+            collective_id=0, has_side_effects=True, vmem_limit_bytes=56 * 1024 * 1024
         ),
         cost_estimate=pl.CostEstimate(
             flops=2 * own * cube * width * (4 * width + 2 * cube),

time: 106 us -> 101 us (0.953)
  Pallas kernels: 102 us -> 98.2 us
    pallas_call x1, Pallas kernels: 102 us -> 98.2 us  [body(): pl.pallas_call(functools.partial(kernel, n_in, n_win, rows, strips), out_...]
    unnamed x5 -> x1, local copies, waits for them, and re-layouts: 3.77 us -> 3.05 us
where the time goes in v2:
time: 101 us
  Pallas kernels  98.2 us (97%)
  local copies, waits for them, and re-layouts  3.05 us (3%)
    pallas_call x1, Pallas kernels, body(): pl.pallas_call(functools.partial(kernel, n_in, n_win, rows, strips), out_...  98.2 us
    unnamed x1, local copies, waits for them, and re-layouts  3.05 us

profile of v2, /device:TPU:0, one launch (start us, length us, event | category | flops | bytes accessed | tf_op | source)
XLA Modules:
  0.0 101.2 jit_solution(9247041769278789158)
XLA Ops:
  0.0 98.2 %shard_map.37 = bf16[2,16,64,512]{3,2,1,0:T(8,128)(2,1)} custom-call(bf16[2,16,64,512]{3,2,1,0:T(8,128)(2,1)} %bitcast.3, bf16[512,1536]{1,0:T(8,128)(2,1)} %w_hbm.1, bf16[512,512]{1,0:T(8,128)(2,1)} %wo_hbm.1), custom_call_target="tpu_custom_call" | custom-call | flops 6442450944 | bytes 4194304 | tf_op jit(solution)/shard_map/pallas_call | solution.py:265
  98.2 3.0 %copy.5 = bf16[2,128,8,512]{3,2,1,0:T(8,128)(2,1)} copy(bf16[2,128,8,512]{3,2,1,0:T(8,128)(2,1)} %bitcast.2) | data formatting | bytes 4194304

commit v3 on v2

--- a/solution.py
+++ b/solution.py
@@ -12,6 +12,7 @@
 HEAD = EMBED_SPAN // FOCUS_GROUPS
 WIN = 8
 EPSILON = 1e-05
+LOG2_E = 1.4426950408889634
 MESH = pl.DeviceIdType.MESH
 F32 = jnp.float32
 BF16 = jnp.bfloat16
@@ -133,6 +134,7 @@
         c_copy(k, d, ii).start()
 
     scale = HEAD ** (-0.5)
+    sharp = scale * LOG2_E
     mine = jnp.dot(cars[ii], w_ref[...], preferred_element_type=F32).astype(BF16)
     kcar_buf[...] = mine[:, width : 2 * width].astype(F32)
     vcar_buf[...] = mine[:, 2 * width :].astype(F32)
@@ -206,8 +208,8 @@
                 s_car = s[tokens : tokens + 1]
                 s = s[:tokens]
                 top = jnp.maximum(jnp.max(s, axis=0, keepdims=True), s_car)
-                e = jnp.exp((s - top) * scale)
-                e_car = jnp.exp((s_car - top) * scale)
+                e = jnp.exp2((s - top) * sharp)
+                e_car = jnp.exp2((s_car - top) * sharp)
                 total = jnp.sum(e, axis=0, keepdims=True) + e_car
                 o = jnp.dot(v_t[lo : lo + HEAD, :], e.astype(BF16), preferred_element_type=F32)
                 o = o + vcar_col[lo : lo + HEAD] * e_car.astype(BF16).astype(F32)
@@ -266,7 +268,7 @@
         functools.partial(kernel, n_in, n_win, rows, strips),
         out_shape=jax.ShapeDtypeStruct(shaped.shape, BF16),
         in_specs=[hbm, hbm, hbm],
-        out_specs=hbm,
+        out_specs=pl.BlockSpec(memory_space=pl.ANY),
         scratch_shapes=[
             pltpu.VMEM((strips,) + block, BF16),
             pltpu.VMEM(w.shape, BF16),
@@ -299,14 +301,14 @@
             dma((2,)),
         ],
         compiler_params=pltpu.CompilerParams(
-            collective_id=0, has_side_effects=True, vmem_limit_bytes=56 * 1024 * 1024
+            collective_id=0, has_side_effects=True, vmem_limit_bytes=36 * 1024 * 1024
         ),
         cost_estimate=pl.CostEstimate(
             flops=2 * own * cube * width * (4 * width + 2 * cube),
             bytes_accessed=4 * own * cube * width,
             transcendentals=own * FOCUS_GROUPS * cube * cube,
         ),
-    )(shaped, w, w_out)
+    )(*(pltpu.with_memory_space_constraint(a, pltpu.HBM) for a in (shaped, w, w_out)))
     return out.reshape(tokens.shape)
 
 

time: 101 us -> 99.5 us (0.985)
  local copies, waits for them, and re-layouts: 3.05 us -> 1.32 us
    unnamed x1, local copies, waits for them, and re-layouts: 3.05 us -> 1.32 us
where the time goes in v3:
time: 99.5 us; the launch traced here: 99.4 us
  Pallas kernels  98 us (98%)
  local copies, waits for them, and re-layouts  1.32 us (1%)
    pallas_call x1, Pallas kernels, body(): pl.pallas_call(functools.partial(kernel, n_in, n_win, rows, strips), out_...  98 us

profile of v3, /device:TPU:0, one launch (start us, length us, event | category | flops | bytes accessed | tf_op | source)
XLA Modules:
  0.0 99.4 jit_solution(17825085454524073165)
XLA Ops:
  0.0 98.0 %shard_map.37 = bf16[2,16,64,512]{3,2,1,0:T(8,128)(2,1)S(1)} custom-call(bf16[2,16,64,512]{3,2,1,0:T(8,128)(2,1)} %bitcast.3, bf16[512,1536]{1,0:T(8,128)(2,1)} %w_hbm.1, bf16[512,512]{1,0:T(8,128)(2,1)} %wo_hbm.1), custom_call_target="tpu_custom_call" | custom-call | flops 6442450944 | bytes 4194304 | tf_op jit(solution)/shard_map/pallas_call | solution.py:267
  98.0 1.3 %copy.5 = bf16[2,128,8,512]{3,2,1,0:T(8,128)(2,1)} copy(bf16[2,128,8,512]{3,2,1,0:T(8,128)(2,1)S(1)} %bitcast.2) | data formatting | bytes 4194304

commit v4 on v3

--- a/solution.py
+++ b/solution.py
@@ -36,7 +36,7 @@
     n_in, n_win, rows, strips,
     tok_ref, w_hbm, wo_hbm, out_ref,
     tok_buf, w_ref, wo_ref,
-    normed, xin, ybuf, psum, cars, wq_t, wv_t, k_buf, q_t, v_t, in_t, glob_buf, kcar_buf, vcar_buf,
+    normed, xin, ybuf, psum, cars, wq_t, wv_t, k_buf, q_t, v_t, in_t, glob_buf, qcar_buf, kcar_buf, vcar_buf,
     fsend, frecv, bsend, brecv, psend, precv, csend, crecv, lsem, blsem, tsem, wsem,
 ):
     ii = lax.axis_index("inline")
@@ -138,21 +138,24 @@
     mine = jnp.dot(cars[ii], w_ref[...], preferred_element_type=F32).astype(BF16)
     kcar_buf[...] = mine[:, width : 2 * width].astype(F32)
     vcar_buf[...] = mine[:, 2 * width :].astype(F32)
-    for d in in_peers:
-        c_copy(0, d, d).wait_recv()
-    every = cars[...].reshape(n_in * group_cars, width)
-    kv = jnp.dot(every, w_ref[:, width:], preferred_element_type=F32).astype(BF16)
-    col_head = lax.broadcasted_iota(jnp.int32, (group_cars, width), 1) // HEAD
-    q_car = mine[:, :width].astype(F32)
-    glob = jnp.zeros((group_cars, width), F32)
-    for h in range(FOCUS_GROUPS):
-        q_h = jnp.where(col_head == h, q_car, 0.0).astype(BF16)
-        s = lax.dot_general(q_h, kv[:, :width], (((1,), (1,)), ((), ())), preferred_element_type=F32) * scale
-        e = jnp.exp(s - jnp.max(s, axis=-1, keepdims=True))
-        t = jnp.sum(e, axis=-1, keepdims=True)
-        o = jnp.dot(e.astype(BF16), kv[:, width:], preferred_element_type=F32) / t
-        glob = jnp.where(col_head == h, o, glob)
-    glob_buf[...] = glob
+    qcar_buf[...] = mine[:, :width].astype(F32)
+
+    def global_part():
+        for d in in_peers:
+            c_copy(0, d, d).wait_recv()
+        every = cars[...].reshape(n_in * group_cars, width)
+        kv = jnp.dot(every, w_ref[:, width:], preferred_element_type=F32).astype(BF16)
+        col_head = lax.broadcasted_iota(jnp.int32, (group_cars, width), 1) // HEAD
+        q_car = qcar_buf[...]
+        glob = jnp.zeros((group_cars, width), F32)
+        for h in range(FOCUS_GROUPS):
+            q_h = jnp.where(col_head == h, q_car, 0.0).astype(BF16)
+            s = lax.dot_general(q_h, kv[:, :width], (((1,), (1,)), ((), ())), preferred_element_type=F32) * scale
+            e = jnp.exp(s - jnp.max(s, axis=-1, keepdims=True))
+            t = jnp.sum(e, axis=-1, keepdims=True)
+            o = jnp.dot(e.astype(BF16), kv[:, width:], preferred_element_type=F32) / t
+            glob = jnp.where(col_head == h, o, glob)
+        glob_buf[...] = glob
 
     def b_copy(slot, p, dst, owner, j):
         return pltpu.make_async_remote_copy(
@@ -164,23 +167,18 @@
     def bl_copy(slot, j):
         return pltpu.make_async_copy(ybuf.at[slot, my_pos], out_ref.at[:, me * span + j], blsem.at[j])
 
-    def cube(slot, carry):
+    halves = 2 if npos % 2 == 0 else 1
+    per = npos // halves
+    queries = tokens // halves
+
+    def half_cube(it, carry):
+        slot = it // halves
         ci = slot // span
         j = lax.rem(slot, span)
-        for p in range(npos):
-            src = ci * npos + p
-
-            @pl.when(src != me)
-            def _():
-                f_copy(0, j, me, src).wait_recv()
-
-            @pl.when(src == me)
-            def _():
-                l_copy(j).wait()
-
-        x = xin[slot].reshape(tokens, width)
+        base = lax.rem(my_pos // per + 1 + lax.rem(it, halves), halves) * per
         row = ci * strips + me * span + j
         pick = lax.broadcasted_iota(jnp.int32, (group_cars, width), 0) == row
+        nt = (((1,), (1,)), ((), ()))
 
         def chosen(ref):
             return jnp.sum(jnp.where(pick, ref[...], 0.0), axis=0, keepdims=True)
@@ -188,12 +186,26 @@
         def column(r):
             return jnp.broadcast_to(r, (128, width)).T[:, :1]
 
-        k_buf[:tokens, :] = jnp.dot(x, w_ref[:, width : 2 * width], preferred_element_type=F32).astype(BF16)
-        k_buf[tokens:, :] = jnp.broadcast_to(chosen(kcar_buf), (16, width)).astype(BF16)
-        nt = (((1,), (1,)), ((), ()))
-        q_t[...] = lax.dot_general(wq_t[...], x, nt, preferred_element_type=F32).astype(BF16)
-        v_t[...] = lax.dot_general(wv_t[...], x, nt, preferred_element_type=F32).astype(BF16)
-        glob_col = column(chosen(glob_buf))
+        @pl.when(lax.rem(it, halves) == 0)
+        def _():
+            for p in range(npos):
+                src = ci * npos + p
+
+                @pl.when(src != me)
+                def _():
+                    f_copy(0, j, me, src).wait_recv()
+
+                @pl.when(src == me)
+                def _():
+                    l_copy(j).wait()
+
+            x = xin[slot].reshape(tokens, width)
+            k_buf[:tokens, :] = jnp.dot(x, w_ref[:, width : 2 * width], preferred_element_type=F32).astype(BF16)
+            k_buf[tokens:, :] = jnp.broadcast_to(chosen(kcar_buf), (16, width)).astype(BF16)
+            v_t[...] = lax.dot_general(wv_t[...], x, nt, preferred_element_type=F32).astype(BF16)
+
+        x_half = xin[slot, pl.ds(base, per)].reshape(queries, width)
+        q_t[...] = lax.dot_general(wq_t[...], x_half, nt, preferred_element_type=F32).astype(BF16)
         vcar_col = column(chosen(vcar_buf))
         for hb in range(width // 128):
             kb = k_buf[:, hb * 128 : (hb + 1) * 128]
@@ -201,9 +213,9 @@
                 lo = hb * 128 + h4 * HEAD
                 parts = [q_t[lo : lo + HEAD, :]]
                 if h4:
-                    parts.insert(0, jnp.zeros((h4 * HEAD, tokens), BF16))
+                    parts.insert(0, jnp.zeros((h4 * HEAD, queries), BF16))
                 if h4 < 128 // HEAD - 1:
-                    parts.append(jnp.zeros((128 - (h4 + 1) * HEAD, tokens), BF16))
+                    parts.append(jnp.zeros((128 - (h4 + 1) * HEAD, queries), BF16))
                 s = jnp.dot(kb, jnp.concatenate(parts, axis=0), preferred_element_type=F32)
                 s_car = s[tokens : tokens + 1]
                 s = s[:tokens]
@@ -213,11 +225,14 @@
                 total = jnp.sum(e, axis=0, keepdims=True) + e_car
                 o = jnp.dot(v_t[lo : lo + HEAD, :], e.astype(BF16), preferred_element_type=F32)
                 o = o + vcar_col[lo : lo + HEAD] * e_car.astype(BF16).astype(F32)
-                in_t[lo : lo + HEAD, :] = (o / total + glob_col[lo : lo + HEAD]).astype(BF16)
-        inner = in_t[...].T
+                in_t[lo : lo + HEAD, :] = o / total
+
+        pl.when(it == 0)(global_part)
+        inner = (in_t[...] + column(chosen(glob_buf))).astype(BF16).T
         upd = jnp.dot(inner, wo_ref[...], preferred_element_type=F32).astype(BF16)
-        ybuf[slot] = upd.reshape(npos, rows, WIN * WIN, width)
-        for p in window_peers(my_pos, npos) + [my_pos]:
+        ybuf[slot, pl.ds(base, per)] = upd.reshape(per, rows, WIN * WIN, width)
+        for o in range(per):
+            p = base + o
             dst = ci * npos + p
 
             @pl.when(dst != me)
@@ -230,7 +245,7 @@
 
         return carry
 
-    lax.fori_loop(0, own, cube, 0)
+    lax.fori_loop(0, own * halves, half_cube, 0)
 
     for k, d in enumerate(peers):
         p_copy(k, d, me).wait_send()
@@ -260,6 +275,7 @@
     own = span * (n_win // npos)
     group_cars = (n_win // npos) * strips
     cube = WIN * WIN * WIN
+    queries = cube // 2 if npos % 2 == 0 else cube
     block = (rows, WIN * WIN, width)
     hbm = pl.BlockSpec(memory_space=pl.ANY)
     dma = pltpu.SemaphoreType.DMA
@@ -281,9 +297,10 @@
             pltpu.VMEM((width, width), BF16),
             pltpu.VMEM((width, width), BF16),
             pltpu.VMEM((cube + 16, width), BF16),
+            pltpu.VMEM((width, queries), BF16),
             pltpu.VMEM((width, cube), BF16),
-            pltpu.VMEM((width, cube), BF16),
-            pltpu.VMEM((width, cube), BF16),
+            pltpu.VMEM((width, queries), F32),
+            pltpu.VMEM((group_cars, width), F32),
             pltpu.VMEM((group_cars, width), F32),
             pltpu.VMEM((group_cars, width), F32),
             pltpu.VMEM((group_cars, width), F32),

time: 99.5 us -> 101 us (1.015)
  Pallas kernels: 98 us -> 99.3 us
    pallas_call x1, Pallas kernels: 98 us -> 99.3 us  [body(): pl.pallas_call(functools.partial(kernel, n_in, n_win, rows, strips), out_...]
where the time goes in v4:
time: 101 us
  Pallas kernels  99.3 us (98%)
  local copies, waits for them, and re-layouts  1.32 us (1%)
    pallas_call x1, Pallas kernels, body(): pl.pallas_call(functools.partial(kernel, n_in, n_win, rows, strips), out_...  99.3 us

profile of v4, /device:TPU:0, one launch (start us, length us, event | category | flops | bytes accessed | tf_op | source)
XLA Modules:
  0.0 100.7 jit_solution(537634144160882787)
XLA Ops:
  0.0 99.3 %shard_map.37 = bf16[2,16,64,512]{3,2,1,0:T(8,128)(2,1)S(1)} custom-call(bf16[2,16,64,512]{3,2,1,0:T(8,128)(2,1)} %bitcast.3, bf16[512,1536]{1,0:T(8,128)(2,1)} %w_hbm.1, bf16[512,512]{1,0:T(8,128)(2,1)} %wo_hbm.1), custom_call_target="tpu_custom_call" | custom-call | flops 6442450944 | bytes 4194304 | tf_op jit(solution)/shard_map/pallas_call | solution.py:283
  99.3 1.3 %copy.5 = bf16[2,128,8,512]{3,2,1,0:T(8,128)(2,1)} copy(bf16[2,128,8,512]{3,2,1,0:T(8,128)(2,1)S(1)} %bitcast.2) | data formatting | bytes 4194304

commit v5 on v3

--- a/solution.py
+++ b/solution.py
@@ -104,12 +104,28 @@
                 f_copy(k, j, d, me).start()
     for k, d in enumerate(peers):
         p_copy(k, d, me).start()
-    for j, k, d in order:
-        if j:
-            if k == len(peers):
-                l_copy(j).start()
-            else:
-                f_copy(k, j, d, me).start()
+
+    def send_round(j):
+        for k, d in enumerate(peers):
+            f_copy(k, j, d, me).start()
+        l_copy(j).start()
+
+    def wait_cube(slot):
+        ci = slot // span
+        j = lax.rem(slot, span)
+        for p in range(npos):
+            src = ci * npos + p
+
+            @pl.when(src != me)
+            def _():
+                f_copy(0, j, me, src).wait_recv()
+
+            @pl.when(src == me)
+            def _():
+                l_copy(j).wait()
+
+    if span > 1:
+        send_round(1)
     w_copy.wait()
     wo_copy.wait()
 
@@ -138,6 +154,9 @@
     mine = jnp.dot(cars[ii], w_ref[...], preferred_element_type=F32).astype(BF16)
     kcar_buf[...] = mine[:, width : 2 * width].astype(F32)
     vcar_buf[...] = mine[:, 2 * width :].astype(F32)
+    wait_cube(jnp.int32(0))
+    if span > 2:
+        send_round(2)
     for d in in_peers:
         c_copy(0, d, d).wait_recv()
     every = cars[...].reshape(n_in * group_cars, width)
@@ -167,16 +186,15 @@
     def cube(slot, carry):
         ci = slot // span
         j = lax.rem(slot, span)
-        for p in range(npos):
-            src = ci * npos + p
-
-            @pl.when(src != me)
-            def _():
-                f_copy(0, j, me, src).wait_recv()
-
-            @pl.when(src == me)
-            def _():
-                l_copy(j).wait()
+        @pl.when(slot > 0)
+        def _():
+            wait_cube(slot)
+
+        for later in range(3, span):
+
+            @pl.when(slot == later - 2)
+            def _():
+                send_round(later)
 
         x = xin[slot].reshape(tokens, width)
         row = ci * strips + me * span + j

time: 99.5 us -> 99.1 us (level)
  no operation moved by 1% of the time
where the time goes in v5:
time: 99.1 us; the launch traced here: 99 us
  Pallas kernels  97.7 us (99%)
  local copies, waits for them, and re-layouts  1.32 us (1%)
    pallas_call x1, Pallas kernels, body(): pl.pallas_call(functools.partial(kernel, n_in, n_win, rows, strips), out_...  97.7 us

profile of v5, /device:TPU:0, one launch (start us, length us, event | category | flops | bytes accessed | tf_op | source)
XLA Modules:
  0.0 99.0 jit_solution(1396701772142248377)
XLA Ops:
  0.0 97.7 %shard_map.37 = bf16[2,16,64,512]{3,2,1,0:T(8,128)(2,1)S(1)} custom-call(bf16[2,16,64,512]{3,2,1,0:T(8,128)(2,1)} %bitcast.3, bf16[512,1536]{1,0:T(8,128)(2,1)} %w_hbm.1, bf16[512,512]{1,0:T(8,128)(2,1)} %wo_hbm.1), custom_call_target="tpu_custom_call" | custom-call | flops 6442450944 | bytes 4194304 | tf_op jit(solution)/shard_map/pallas_call | solution.py:285
  97.7 1.3 %copy.5 = bf16[2,128,8,512]{3,2,1,0:T(8,128)(2,1)} copy(bf16[2,128,8,512]{3,2,1,0:T(8,128)(2,1)S(1)} %bitcast.2) | data formatting | bytes 4194304

commit v6 on v3

--- a/solution.py
+++ b/solution.py
@@ -36,8 +36,8 @@
     n_in, n_win, rows, strips,
     tok_ref, w_hbm, wo_hbm, out_ref,
     tok_buf, w_ref, wo_ref,
-    normed, xin, ybuf, psum, cars, wq_t, wv_t, k_buf, q_t, v_t, in_t, glob_buf, kcar_buf, vcar_buf,
-    fsend, frecv, bsend, brecv, psend, precv, csend, crecv, lsem, blsem, tsem, wsem,
+    normed, xin, ybuf, psum, own_cars, all_cars, cars, wq_t, wv_t, k_buf, q_t, v_t, in_t, glob_buf, kcar_buf, vcar_buf,
+    fsend, frecv, bsend, brecv, psend, precv, gsend, grecv, csend, crecv, lsem, blsem, tsem, wsem,
 ):
     ii = lax.axis_index("inline")
     me = lax.axis_index("window")
@@ -74,7 +74,7 @@
 
     def p_copy(k, d, src):
         return pltpu.make_async_remote_copy(
-            src_ref=psum.at[src], dst_ref=psum.at[src], send_sem=psend.at[k], recv_sem=precv.at[src],
+            src_ref=psum.at[src, d], dst_ref=psum.at[src, d], send_sem=psend.at[k], recv_sem=precv.at[src],
             device_id={"window": d}, device_id_type=MESH,
         )
 
@@ -94,7 +94,7 @@
         t_copy(n).wait()
         x = standardize(tok_buf[n].astype(F32)).astype(BF16)
         normed[d * span + j] = x
-        psum[me, pl.ds(d * span + j, 1), :] = jnp.sum(x.astype(F32), axis=(0, 1))[None, :]
+        psum[me, d, pl.ds(j, 1), :] = jnp.sum(x.astype(F32), axis=(0, 1))[None, :]
         if n == 0:
             pl.semaphore_wait(barrier, len(peers) + len(in_peers))
         if j == 0:
@@ -104,25 +104,44 @@
                 f_copy(k, j, d, me).start()
     for k, d in enumerate(peers):
         p_copy(k, d, me).start()
-    for j, k, d in order:
-        if j:
-            if k == len(peers):
-                l_copy(j).start()
-            else:
-                f_copy(k, j, d, me).start()
+
+    def send_round(j):
+        for k, d in enumerate(peers):
+            f_copy(k, j, d, me).start()
+        l_copy(j).start()
+
+    if span > 1:
+        send_round(1)
     w_copy.wait()
     wo_copy.wait()
 
     wq_t[...] = w_ref[:, :width].T
     wv_t[...] = w_ref[:, 2 * width :].T
 
+    def g_copy(k, d, src):
+        return pltpu.make_async_remote_copy(
+            src_ref=own_cars.at[src], dst_ref=own_cars.at[src], send_sem=gsend.at[k], recv_sem=grecv.at[src],
+            device_id={"window": d}, device_id_type=MESH,
+        )
+
     for d in peers:
-        p_copy(0, d, d).wait_recv()
+        p_copy(0, me, d).wait_recv()
     for ci in range(n_ci):
-        total = psum[ci * npos]
+        total = psum[ci * npos, me]
         for p in range(1, npos):
-            total = total + psum[ci * npos + p]
-        cars[ii, pl.ds(ci * strips, strips), :] = standardize(total * (1.0 / tokens)).astype(BF16)
+            total = total + psum[ci * npos + p, me]
+        own_cars[me, ci] = standardize(total * (1.0 / tokens))
+    for k, d in enumerate(peers):
+        g_copy(k, d, me).start()
+    for j in range(2, span):
+        send_round(j)
+    for d in peers:
+        g_copy(0, me, d).wait_recv()
+    for ci in range(n_ci):
+        for w in range(n_win):
+            first = ci * strips + w * span
+            all_cars[first : first + span, :] = own_cars[w, ci]
+    cars[ii] = all_cars[...].astype(BF16)
 
     def c_copy(k, d, src):
         return pltpu.make_async_remote_copy(
@@ -217,7 +236,7 @@
         inner = in_t[...].T
         upd = jnp.dot(inner, wo_ref[...], preferred_element_type=F32).astype(BF16)
         ybuf[slot] = upd.reshape(npos, rows, WIN * WIN, width)
-        for p in window_peers(my_pos, npos) + [my_pos]:
+        for p in reversed(window_peers(my_pos, npos) + [my_pos]):
             dst = ci * npos + p
 
             @pl.when(dst != me)
@@ -234,6 +253,7 @@
 
     for k, d in enumerate(peers):
         p_copy(k, d, me).wait_send()
+        g_copy(k, d, me).wait_send()
     for k, d in enumerate(in_peers):
         c_copy(k, d, ii).wait_send()
     for j in range(span):
@@ -276,7 +296,9 @@
             pltpu.VMEM((strips,) + block, BF16),
             pltpu.VMEM((own, npos) + block, BF16),
             pltpu.VMEM((own, npos) + block, BF16),
-            pltpu.VMEM((n_win, strips, width), F32),
+            pltpu.VMEM((n_win, n_win, span, width), F32),
+            pltpu.VMEM((n_win, n_win // npos, span, width), F32),
+            pltpu.VMEM((group_cars, width), F32),
             pltpu.VMEM((n_in, group_cars, width), BF16),
             pltpu.VMEM((width, width), BF16),
             pltpu.VMEM((width, width), BF16),
@@ -291,6 +313,8 @@
             dma((n_win, span)),
             dma((own, npos)),
             dma((n_win, span)),
+            dma((n_win,)),
+            dma((n_win,)),
             dma((n_win,)),
             dma((n_win,)),
             dma((n_in,)),

time: 99.5 us -> 104 us (1.045)
  Pallas kernels: 98 us -> 102 us
    pallas_call x1, Pallas kernels: 98 us -> 102 us  [body(): pl.pallas_call(functools.partial(kernel, n_in, n_win, rows, strips), out_...]
where the time goes in v6:
time: 104 us; the launch traced here: 103 us
  Pallas kernels  102 us (98%)
  local copies, waits for them, and re-layouts  1.32 us (1%)
    pallas_call x1, Pallas kernels, body(): pl.pallas_call(functools.partial(kernel, n_in, n_win, rows, strips), out_...  102 us

profile of v6, /device:TPU:0, one launch (start us, length us, event | category | flops | bytes accessed | tf_op | source)
XLA Modules:
  0.0 103.5 jit_solution(12170924425786931665)
XLA Ops:
  0.0 102.1 %shard_map.37 = bf16[2,16,64,512]{3,2,1,0:T(8,128)(2,1)S(1)} custom-call(bf16[2,16,64,512]{3,2,1,0:T(8,128)(2,1)} %bitcast.3, bf16[512,1536]{1,0:T(8,128)(2,1)} %w_hbm.1, bf16[512,512]{1,0:T(8,128)(2,1)} %wo_hbm.1), custom_call_target="tpu_custom_call" | custom-call | flops 6442450944 | bytes 4194304 | tf_op jit(solution)/shard_map/pallas_call | solution.py:287
  102.2 1.3 %copy.5 = bf16[2,128,8,512]{3,2,1,0:T(8,128)(2,1)} copy(bf16[2,128,8,512]{3,2,1,0:T(8,128)(2,1)S(1)} %bitcast.2) | data formatting | bytes 4194304

commit v7 on v3

--- a/solution.py
+++ b/solution.py
@@ -36,7 +36,7 @@
     n_in, n_win, rows, strips,
     tok_ref, w_hbm, wo_hbm, out_ref,
     tok_buf, w_ref, wo_ref,
-    normed, xin, ybuf, psum, cars, wq_t, wv_t, k_buf, q_t, v_t, in_t, glob_buf, kcar_buf, vcar_buf,
+    normed, xin, ybuf, psum, cars, wq_t, wv_t, k_buf, q_t, v_t, in_t, glob_buf, qcar_buf, kcar_buf, vcar_buf,
     fsend, frecv, bsend, brecv, psend, precv, csend, crecv, lsem, blsem, tsem, wsem,
 ):
     ii = lax.axis_index("inline")
@@ -138,21 +138,24 @@
     mine = jnp.dot(cars[ii], w_ref[...], preferred_element_type=F32).astype(BF16)
     kcar_buf[...] = mine[:, width : 2 * width].astype(F32)
     vcar_buf[...] = mine[:, 2 * width :].astype(F32)
-    for d in in_peers:
-        c_copy(0, d, d).wait_recv()
-    every = cars[...].reshape(n_in * group_cars, width)
-    kv = jnp.dot(every, w_ref[:, width:], preferred_element_type=F32).astype(BF16)
-    col_head = lax.broadcasted_iota(jnp.int32, (group_cars, width), 1) // HEAD
-    q_car = mine[:, :width].astype(F32)
-    glob = jnp.zeros((group_cars, width), F32)
-    for h in range(FOCUS_GROUPS):
-        q_h = jnp.where(col_head == h, q_car, 0.0).astype(BF16)
-        s = lax.dot_general(q_h, kv[:, :width], (((1,), (1,)), ((), ())), preferred_element_type=F32) * scale
-        e = jnp.exp(s - jnp.max(s, axis=-1, keepdims=True))
-        t = jnp.sum(e, axis=-1, keepdims=True)
-        o = jnp.dot(e.astype(BF16), kv[:, width:], preferred_element_type=F32) / t
-        glob = jnp.where(col_head == h, o, glob)
-    glob_buf[...] = glob
+    qcar_buf[...] = mine[:, :width].astype(F32)
+
+    def global_part():
+        for d in in_peers:
+            c_copy(0, d, d).wait_recv()
+        every = cars[...].reshape(n_in * group_cars, width)
+        kv = jnp.dot(every, w_ref[:, width:], preferred_element_type=F32).astype(BF16)
+        col_head = lax.broadcasted_iota(jnp.int32, (group_cars, width), 1) // HEAD
+        q_car = qcar_buf[...]
+        glob = jnp.zeros((group_cars, width), F32)
+        for h in range(FOCUS_GROUPS):
+            q_h = jnp.where(col_head == h, q_car, 0.0).astype(BF16)
+            s = lax.dot_general(q_h, kv[:, :width], (((1,), (1,)), ((), ())), preferred_element_type=F32) * scale
+            e = jnp.exp(s - jnp.max(s, axis=-1, keepdims=True))
+            t = jnp.sum(e, axis=-1, keepdims=True)
+            o = jnp.dot(e.astype(BF16), kv[:, width:], preferred_element_type=F32) / t
+            glob = jnp.where(col_head == h, o, glob)
+        glob_buf[...] = glob
 
     def b_copy(slot, p, dst, owner, j):
         return pltpu.make_async_remote_copy(
@@ -193,7 +196,6 @@
         nt = (((1,), (1,)), ((), ()))
         q_t[...] = lax.dot_general(wq_t[...], x, nt, preferred_element_type=F32).astype(BF16)
         v_t[...] = lax.dot_general(wv_t[...], x, nt, preferred_element_type=F32).astype(BF16)
-        glob_col = column(chosen(glob_buf))
         vcar_col = column(chosen(vcar_buf))
         for hb in range(width // 128):
             kb = k_buf[:, hb * 128 : (hb + 1) * 128]
@@ -210,11 +212,14 @@
                 top = jnp.maximum(jnp.max(s, axis=0, keepdims=True), s_car)
                 e = jnp.exp2((s - top) * sharp)
                 e_car = jnp.exp2((s_car - top) * sharp)
-                total = jnp.sum(e, axis=0, keepdims=True) + e_car
-                o = jnp.dot(v_t[lo : lo + HEAD, :], e.astype(BF16), preferred_element_type=F32)
-                o = o + vcar_col[lo : lo + HEAD] * e_car.astype(BF16).astype(F32)
-                in_t[lo : lo + HEAD, :] = (o / total + glob_col[lo : lo + HEAD]).astype(BF16)
-        inner = in_t[...].T
+                v_one = jnp.concatenate([v_t[lo : lo + HEAD, :], jnp.ones((16, tokens), BF16)], axis=0)
+                o = jnp.dot(v_one, e.astype(BF16), preferred_element_type=F32)
+                total = o[HEAD : HEAD + 1] + e_car
+                o = o[:HEAD] + vcar_col[lo : lo + HEAD] * e_car.astype(BF16).astype(F32)
+                in_t[lo : lo + HEAD, :] = o / total
+
+        pl.when(slot == 0)(global_part)
+        inner = (in_t[...] + column(chosen(glob_buf))).astype(BF16).T
         upd = jnp.dot(inner, wo_ref[...], preferred_element_type=F32).astype(BF16)
         ybuf[slot] = upd.reshape(npos, rows, WIN * WIN, width)
         for p in window_peers(my_pos, npos) + [my_pos]:
@@ -283,7 +288,8 @@
             pltpu.VMEM((cube + 16, width), BF16),
             pltpu.VMEM((width, cube), BF16),
             pltpu.VMEM((width, cube), BF16),
-            pltpu.VMEM((width, cube), BF16),
+            pltpu.VMEM((width, cube), F32),
+            pltpu.VMEM((group_cars, width), F32),
             pltpu.VMEM((group_cars, width), F32),
             pltpu.VMEM((group_cars, width), F32),
             pltpu.VMEM((group_cars, width), F32),

time: 99.5 us -> 99.5 us (level)
  no operation moved by 1% of the time
where the time goes in v7:
time: 99.5 us; the launch traced here: 99.3 us
  Pallas kernels  98 us (98%)
  local copies, waits for them, and re-layouts  1.32 us (1%)
    pallas_call x1, Pallas kernels, body(): pl.pallas_call(functools.partial(kernel, n_in, n_win, rows, strips), out_...  98 us

profile of v7, /device:TPU:0, one launch (start us, length us, event | category | flops | bytes accessed | tf_op | source)
XLA Modules:
  0.0 99.3 jit_solution(12439688059543583818)
XLA Ops:
  0.0 98.0 %shard_map.37 = bf16[2,16,64,512]{3,2,1,0:T(8,128)(2,1)S(1)} custom-call(bf16[2,16,64,512]{3,2,1,0:T(8,128)(2,1)} %bitcast.3, bf16[512,1536]{1,0:T(8,128)(2,1)} %w_hbm.1, bf16[512,512]{1,0:T(8,128)(2,1)} %wo_hbm.1), custom_call_target="tpu_custom_call" | custom-call | flops 6442450944 | bytes 4194304 | tf_op jit(solution)/shard_map/pallas_call | solution.py:272
  98.0 1.3 %copy.5 = bf16[2,128,8,512]{3,2,1,0:T(8,128)(2,1)} copy(bf16[2,128,8,512]{3,2,1,0:T(8,128)(2,1)S(1)} %bitcast.2) | data formatting | bytes 4194304

commit v8 on v7

--- a/solution.py
+++ b/solution.py
@@ -36,8 +36,8 @@
     n_in, n_win, rows, strips,
     tok_ref, w_hbm, wo_hbm, out_ref,
     tok_buf, w_ref, wo_ref,
-    normed, xin, ybuf, psum, cars, wq_t, wv_t, k_buf, q_t, v_t, in_t, glob_buf, qcar_buf, kcar_buf, vcar_buf,
-    fsend, frecv, bsend, brecv, psend, precv, csend, crecv, lsem, blsem, tsem, wsem,
+    normed, xin, ybuf, psum, own_cars, all_cars, cars, wq_t, wv_t, k_buf, q_t, v_t, in_t, glob_buf, qcar_buf, kcar_buf, vcar_buf,
+    fsend, frecv, bsend, brecv, psend, precv, gsend, grecv, csend, crecv, lsem, blsem, tsem, wsem,
 ):
     ii = lax.axis_index("inline")
     me = lax.axis_index("window")
@@ -74,7 +74,7 @@
 
     def p_copy(k, d, src):
         return pltpu.make_async_remote_copy(
-            src_ref=psum.at[src], dst_ref=psum.at[src], send_sem=psend.at[k], recv_sem=precv.at[src],
+            src_ref=psum.at[src, d], dst_ref=psum.at[src, d], send_sem=psend.at[k], recv_sem=precv.at[src],
             device_id={"window": d}, device_id_type=MESH,
         )
 
@@ -94,7 +94,7 @@
         t_copy(n).wait()
         x = standardize(tok_buf[n].astype(F32)).astype(BF16)
         normed[d * span + j] = x
-        psum[me, pl.ds(d * span + j, 1), :] = jnp.sum(x.astype(F32), axis=(0, 1))[None, :]
+        psum[me, d, pl.ds(j, 1), :] = jnp.sum(x.astype(F32), axis=(0, 1))[None, :]
         if n == 0:
             pl.semaphore_wait(barrier, len(peers) + len(in_peers))
         if j == 0:
@@ -104,25 +104,44 @@
                 f_copy(k, j, d, me).start()
     for k, d in enumerate(peers):
         p_copy(k, d, me).start()
-    for j, k, d in order:
-        if j:
-            if k == len(peers):
-                l_copy(j).start()
-            else:
-                f_copy(k, j, d, me).start()
+
+    def send_round(j):
+        for k, d in enumerate(peers):
+            f_copy(k, j, d, me).start()
+        l_copy(j).start()
+
+    if span > 1:
+        send_round(1)
     w_copy.wait()
     wo_copy.wait()
 
     wq_t[...] = w_ref[:, :width].T
     wv_t[...] = w_ref[:, 2 * width :].T
 
+    def g_copy(k, d, src):
+        return pltpu.make_async_remote_copy(
+            src_ref=own_cars.at[src], dst_ref=own_cars.at[src], send_sem=gsend.at[k], recv_sem=grecv.at[src],
+            device_id={"window": d}, device_id_type=MESH,
+        )
+
     for d in peers:
-        p_copy(0, d, d).wait_recv()
+        p_copy(0, me, d).wait_recv()
     for ci in range(n_ci):
-        total = psum[ci * npos]
+        total = psum[ci * npos, me]
         for p in range(1, npos):
-            total = total + psum[ci * npos + p]
-        cars[ii, pl.ds(ci * strips, strips), :] = standardize(total * (1.0 / tokens)).astype(BF16)
+            total = total + psum[ci * npos + p, me]
+        own_cars[me, ci] = standardize(total * (1.0 / tokens))
+    for k, d in enumerate(peers):
+        g_copy(k, d, me).start()
+    for j in range(2, span):
+        send_round(j)
+    for d in peers:
+        g_copy(0, me, d).wait_recv()
+    for ci in range(n_ci):
+        for w in range(n_win):
+            first = ci * strips + w * span
+            all_cars[first : first + span, :] = own_cars[w, ci]
+    cars[ii] = all_cars[...].astype(BF16)
 
     def c_copy(k, d, src):
         return pltpu.make_async_remote_copy(
@@ -239,6 +258,7 @@
 
     for k, d in enumerate(peers):
         p_copy(k, d, me).wait_send()
+        g_copy(k, d, me).wait_send()
     for k, d in enumerate(in_peers):
         c_copy(k, d, ii).wait_send()
     for j in range(span):
@@ -281,7 +301,9 @@
             pltpu.VMEM((strips,) + block, BF16),
             pltpu.VMEM((own, npos) + block, BF16),
             pltpu.VMEM((own, npos) + block, BF16),
-            pltpu.VMEM((n_win, strips, width), F32),
+            pltpu.VMEM((n_win, n_win, span, width), F32),
+            pltpu.VMEM((n_win, n_win // npos, span, width), F32),
+            pltpu.VMEM((group_cars, width), F32),
             pltpu.VMEM((n_in, group_cars, width), BF16),
             pltpu.VMEM((width, width), BF16),
             pltpu.VMEM((width, width), BF16),
@@ -297,6 +319,8 @@
             dma((n_win, span)),
             dma((own, npos)),
             dma((n_win, span)),
+            dma((n_win,)),
+            dma((n_win,)),
             dma((n_win,)),
             dma((n_win,)),
             dma((n_in,)),

time: 99.5 us -> 100 us (level)
  no operation moved by 1% of the time
where the time goes in v8:
time: 100 us; the launch traced here: 99.9 us
  Pallas kernels  98.5 us (98%)
  local copies, waits for them, and re-layouts  1.32 us (1%)
    pallas_call x1, Pallas kernels, body(): pl.pallas_call(functools.partial(kernel, n_in, n_win, rows, strips), out_...  98.5 us

profile of v8, /device:TPU:0, one launch (start us, length us, event | category | flops | bytes accessed | tf_op | source)
XLA Modules:
  0.0 99.9 jit_solution(4027262785821659942)
XLA Ops:
  0.0 98.5 %shard_map.37 = bf16[2,16,64,512]{3,2,1,0:T(8,128)(2,1)S(1)} custom-call(bf16[2,16,64,512]{3,2,1,0:T(8,128)(2,1)} %bitcast.3, bf16[512,1536]{1,0:T(8,128)(2,1)} %w_hbm.1, bf16[512,512]{1,0:T(8,128)(2,1)} %wo_hbm.1), custom_call_target="tpu_custom_call" | custom-call | flops 6442450944 | bytes 4194304 | tf_op jit(solution)/shard_map/pallas_call | solution.py:292
  98.5 1.3 %copy.5 = bf16[2,128,8,512]{3,2,1,0:T(8,128)(2,1)} copy(bf16[2,128,8,512]{3,2,1,0:T(8,128)(2,1)S(1)} %bitcast.2) | data formatting | bytes 4194304
